TPU v7x, 256 devices: a whole 4x4x8 slice. The times are simulated.
256 devices in a mesh: expert: 8 (over y, core), fsdp: 32 (over x, z).
Axes of the slice: x: 4, y: 4, z: 8, core: 2. Of those that a mesh axis runs over, the one named last changes fastest.
Arguments:
- tokens: bfloat16 [32768, 3072], P(('expert', 'fsdp')), may hold values from -6 to 6
- cotangent: bfloat16 [32768, 3072], P(('expert', 'fsdp')), may hold values from -6 to 6
- expert_ids: int32 [32768, 2], P(('expert', 'fsdp')), may hold values from 0 to 7, all different within a row; in each aligned block of 128 rows (0 to 127, 128 to 255, ...) at most 40 rows name the same one
- probs: bfloat16 [32768, 2], P(('expert', 'fsdp')), may hold values from 0.049804688 to 0.94921875
- gate_tiles: bfloat16 [8, 32, 128, 128], P('expert', 'fsdp'), may hold values from -0.5 to 0.5
- up_tiles: bfloat16 [8, 32, 128, 128], P('expert', 'fsdp'), may hold values from -0.5 to 0.5
- down_tiles: bfloat16 [8, 32, 128, 128], P('expert', 'fsdp'), may hold values from -0.5 to 0.5
- in_ids: int32 [8, 32], P('expert'), may hold values from 0 to 1535, as said below
- in_count: int32 [8, 32], P('expert'), may hold values from 0 to 1, as said below
- out_ids: int32 [8, 32], P('expert'), may hold values from 0 to 23
- out_count: int32 [8, 32], P('expert'), may hold values from 0 to 1, as said below
Outputs:
- token_grad: bfloat16 [32768, 3072], P(('expert', 'fsdp'))
- prob_grad: bfloat16 [32768, 2], P(('expert', 'fsdp'))
- gate_grad: float32 [8, 32, 128, 128], P('expert', 'fsdp')
- up_grad: float32 [8, 32, 128, 128], P('expert', 'fsdp')
- down_grad: float32 [8, 32, 128, 128], P('expert', 'fsdp')
Inputs may be any that keep to these rules, and one draw needn't show every extreme that they name: `expert_ids`: in each block of the rows of one device no expert is named more than 40 times. The column blocks in_ids % (64) of the 32 entries of one expert differ from one another. `in_count`: some device of each expert has all its slots live. `out_count`: some device of each expert has all its slots live.
All inputs are finite; a program needn't handle non-finite values.
Results may differ from a plain program's by a relative error of at most 0.0052.
Values may be sent and summed in bfloat16 or wider, within the bound.
No kernel may reach another device: no remote copies, remote signals or barrier semaphores. Data moves between devices by JAX's collectives and lax.ppermute only.
A program may use at most 128 MiB of HBM per device.

v0:
```python
import jax
import jax.numpy as jnp
from jax import lax
from jax.sharding import PartitionSpec as P

FF = 8192


def slot_positions(block_ids, experts, capacity):
    flat = block_ids.reshape(-1)
    onehot = (flat[:, None] == jnp.arange(experts, dtype=jnp.int32)[None, :]).astype(jnp.int32)
    before = jnp.cumsum(onehot, axis=0) - onehot
    return flat * capacity + jnp.sum(before * onehot, axis=1)


def place_terms(terms, index_to, blocks):
    return jnp.zeros((blocks,) + terms.shape[1:], jnp.float32).at[index_to].add(terms)


def forward_product(picked, tiles):
    return jnp.einsum("sri,sij->srj", picked, tiles, preferred_element_type=jnp.float32)


def backward_product(picked, tiles):
    return jnp.einsum("srj,sij->sri", picked, tiles, preferred_element_type=jnp.float32)


def tile_product(left, right):
    return jnp.einsum("sri,srj->sij", left, right, preferred_element_type=jnp.float32)


def live_slots(counts, per_device):
    return (jnp.arange(per_device, dtype=jnp.int32)[None, :] < counts[:, None]).reshape(-1)


def local(
    tokens,
    cotangent,
    expert_ids,
    probs,
    gate_tiles,
    up_tiles,
    down_tiles,
    in_ids,
    in_count,
    out_ids,
    out_count,
):
    rows, width = tokens.shape
    top = expert_ids.shape[1]
    groups = lax.axis_size("expert")
    capacity = rows * top * 5 // (groups * 4)
    per_device = gate_tiles.shape[1]
    tile = gate_tiles.shape[2]
    col_blocks = FF // tile
    row_blocks = width // tile
    count = rows * top
    total = groups * capacity
    positions = slot_positions(expert_ids, groups, capacity)
    table = (
        jnp.full((total,), count, jnp.int32).at[positions].set(jnp.arange(count, dtype=jnp.int32))
    )
    token_of = table // top

    def spread(values):
        padded = jnp.concatenate([values, jnp.zeros((1, width), values.dtype)], axis=0)
        blocked = padded.reshape(rows + 1, row_blocks, tile).transpose(1, 0, 2)
        return jnp.take(blocked, token_of, axis=1).reshape(row_blocks, groups, capacity, tile)

    prob_pad = jnp.concatenate([probs.reshape(-1), jnp.zeros((1,), probs.dtype)])
    send_p = jnp.take(prob_pad, table, axis=0).reshape(1, groups, capacity)
    got_x, got_dy, got_p = (
        lax.all_to_all(spread(tokens), "expert", split_axis=1, concat_axis=1, tiled=True),
        lax.all_to_all(spread(cotangent), "expert", split_axis=1, concat_axis=1, tiled=True),
        lax.all_to_all(send_p, "expert", split_axis=1, concat_axis=1, tiled=True),
    )
    x_t = got_x.reshape(row_blocks, total, tile)
    dy_t = got_dy.reshape(row_blocks, total, tile)
    p_rows = got_p.reshape(1, total, 1).astype(jnp.float32)
    gate_all, up_all, down_all = (
        lax.all_gather(gate_tiles, "fsdp", axis=1, tiled=True),
        lax.all_gather(up_tiles, "fsdp", axis=1, tiled=True),
        lax.all_gather(down_tiles, "fsdp", axis=1, tiled=True),
    )
    live_in = live_slots(in_count[0], per_device)
    live_out = live_slots(out_count[0], per_device)
    in_mask = live_in.astype(jnp.bfloat16)[:, None, None]
    gate = gate_all[0] * in_mask
    up = up_all[0] * in_mask
    in_row = in_ids[0] // col_blocks
    out_col = out_ids[0]
    x_sel = jnp.take(x_t, in_row, axis=0)
    g = forward_product(x_sel, gate)
    u = forward_product(x_sel, up)
    sig = jax.nn.sigmoid(g)
    act = g * sig
    hidden = (act * u).astype(jnp.bfloat16)
    down = down_all[0] * live_out.astype(jnp.bfloat16)[:, None, None]
    scaled = (p_rows * dy_t.astype(jnp.float32)).astype(jnp.bfloat16)
    down_part = (
        tile_product(hidden, jnp.take(scaled, out_col, axis=0))
        * live_out.astype(jnp.float32)[:, None, None]
    )
    m = backward_product(jnp.take(dy_t, out_col, axis=0), down)
    out_rows = place_terms(forward_product(hidden, down), out_col, row_blocks)
    prob_rows = jnp.sum(dy_t.astype(jnp.float32) * out_rows, axis=(0, 2))
    dh = p_rows * m
    dg = (dh * u * sig * (1.0 + g * (1.0 - sig))).astype(jnp.bfloat16)
    du = (dh * act).astype(jnp.bfloat16)
    both = backward_product(dg, gate) + backward_product(du, up)
    part = place_terms(both, in_row, row_blocks).astype(jnp.bfloat16)
    in_live = live_in.astype(jnp.float32)[:, None, None]
    gate_part = tile_product(x_sel, dg) * in_live
    up_part = tile_product(x_sel, du) * in_live
    back_x, back_p = (
        lax.all_to_all(
            part.reshape(row_blocks, groups, capacity, tile),
            "expert",
            split_axis=1,
            concat_axis=1,
            tiled=True,
        ),
        lax.all_to_all(
            prob_rows.astype(jnp.bfloat16).reshape(1, groups, capacity),
            "expert",
            split_axis=1,
            concat_axis=1,
            tiled=True,
        ),
    )
    gate_grad, up_grad, down_grad = (
        lax.psum_scatter(gate_part, "fsdp", scatter_dimension=0, tiled=True),
        lax.psum_scatter(up_part, "fsdp", scatter_dimension=0, tiled=True),
        lax.psum_scatter(down_part, "fsdp", scatter_dimension=0, tiled=True),
    )
    picked = jnp.take(back_x.reshape(row_blocks, total, tile), positions, axis=1).reshape(
        row_blocks, rows, top, tile
    )
    token_grad = (
        jnp.sum(picked.astype(jnp.float32), axis=2)
        .transpose(1, 0, 2)
        .reshape(rows, width)
        .astype(jnp.bfloat16)
    )
    prob_grad = jnp.take(back_p.reshape(-1), positions, axis=0).reshape(rows, top)
    return (token_grad, prob_grad, gate_grad[None], up_grad[None], down_grad[None])


def solution(mesh):
    return jax.shard_map(
        local,
        mesh=mesh,
        in_specs=(
            P(("expert", "fsdp"), None),
            P(("expert", "fsdp"), None),
            P(("expert", "fsdp"), None),
            P(("expert", "fsdp"), None),
            P("expert", "fsdp", None, None),
            P("expert", "fsdp", None, None),
            P("expert", "fsdp", None, None),
            P("expert", None),
            P("expert", None),
            P("expert", None),
            P("expert", None),
        ),
        out_specs=(
            P(("expert", "fsdp"), None),
            P(("expert", "fsdp"), None),
            P("expert", "fsdp", None, None),
            P("expert", "fsdp", None, None),
            P("expert", "fsdp", None, None),
        ),
        check_vma=False,
    )
```

profile of v0, /device:TPU:32, one launch (start us, length us, event | category | flops | bytes accessed | tf_op | source)
XLA Modules:
  0.0 913.0 jit_solution(11741230452350666648)
XLA Ops:
  16.2 4.5 all-to-all-start
  34.6 4.8 all-to-all-start.1
  43.3 21.9 %all-to-all-done.1 = bf16[24,8,40,128]{3,2,0,1:T(8,128)(2,1)S(1)} async-done(((bf16[24,8,40,128]{3,2,0,1:T(8,128)(2,1)}), bf16[24,8,40,128]{3,2,0,1:T(8,128)(2,1)S(1)}, u32[]{:S(2)}, u32[]{:S(2)}) %all-to-all-start.1) | async-done | bytes 1966112 | tf_op jit(solution)/shard_map/all_to_all | solution.py:74
  65.3 4.3 all-to-all-start.2
  77.2 3.9 gather_fusion.7
  81.1 14.3 %all-to-all-done.2 = bf16[24,8,40,128]{3,2,0,1:T(8,128)(2,1)} async-done(((bf16[24,8,40,128]{3,2,0,1:T(8,128)(2,1)}), bf16[24,8,40,128]{3,2,0,1:T(8,128)(2,1)}, u32[]{:S(2)}, u32[]{:S(2)}) %all-to-all-start.2) | async-done | bytes 1966112 | tf_op jit(solution)/shard_map/all_to_all | solution.py:73
  95.4 3.4 copy.71
  98.8 3.9 gather_fusion.6
  102.7 5.3 fusion.15
  107.9 56.9 %all-gather.8.cloned.1.call-done = bf16[1,32,128,128]{3,2,0,1:T(8,128)(2,1)} async-done(((bf16[1,1,128,128]{3,2,0,1:T(8,128)(2,1)}), bf16[1,32,128,128]{3,2,0,1:T(8,128)(2,1)}) %all-gather.8.cloned.1.call-update) | async-done | bytes 1048592 | tf_op jit(solution)/shard_map/all_gather | solution.py:81
  164.8 5.2 fusion.17
  170.1 71.1 %all-gather.4.cloned.1.call-done = bf16[1,32,128,128]{3,2,0,1:T(8,128)(2,1)} async-done(((bf16[1,1,128,128]{3,2,0,1:T(8,128)(2,1)}), bf16[1,32,128,128]{3,2,0,1:T(8,128)(2,1)}) %all-gather.4.cloned.1.call-update) | async-done | bytes 1048592 | tf_op jit(solution)/shard_map/all_gather | solution.py:83
  241.2 8.7 multiply_convert_fusion.1
  254.0 5.0 convolution_multiply_fusion.1
  259.3 5.0 convolution_multiply_fusion
  265.6 4.9 fusion.14
  272.9 11.2 %scatter_fusion.1 = f32[24,320,128]{2,1,0:T(8,128)} fusion(f32[24,320,128]{2,1,0:T(8,128)} %broadcast.207.clone, s32[32]{0:T(128)S(1)} %fusion.36, f32[32,320,128]{2,1,0:T(8,128)} %fusion.14), kind=kCustom, calls=%fused_computation.10 | custom fusion | flops 1310720 | bytes 15728768 | tf_op jit(solution)/shard_map/scatter-add | solution.py:17
  287.5 4.4 all-to-all-start.4
  300.3 11.4 %scatter_fusion = f32[24,320,128]{2,1,0:T(8,128)} fusion(f32[24,320,128]{2,1,0:T(8,128)} %broadcast.207.clone.1, s32[32]{0:T(128)S(1)} %fusion.35, f32[32,320,128]{2,1,0:T(8,128)} %convolution_add_fusion), kind=kCustom, calls=%fused_computation.9 | custom fusion | flops 1310720 | bytes 15728768 | tf_op jit(solution)/shard_map/scatter-add | solution.py:17
  315.9 5.0 all-to-all-start.3
  323.9 22.8 %all-to-all-done.3 = bf16[24,8,40,128]{3,2,0,1:T(8,128)(2,1)S(1)} async-done(((bf16[24,8,40,128]{3,2,0,1:T(8,128)(2,1)}), bf16[24,8,40,128]{3,2,0,1:T(8,128)(2,1)S(1)}, u32[]{:S(2)}, u32[]{:S(2)}) %all-to-all-start.3) | async-done | bytes 1966112 | tf_op jit(solution)/shard_map/all_to_all | solution.py:116
  352.7 115.4 %reduce-scatter.8.cloned.1.call-done = f32[1,128,128]{2,1,0:T(8,128)} async-done(((f32[32,128,128]{2,1,0:T(8,128)}), f32[1,128,128]{2,1,0:T(8,128)}) %reduce-scatter.8.cloned.1.call-update) | async-done | bytes 65552 | tf_op jit(solution)/shard_map/reduce_scatter | solution.py:134
  468.0 219.3 %reduce-scatter.4.cloned.1.call-done = f32[1,128,128]{2,1,0:T(8,128)} async-done(((f32[32,128,128]{2,1,0:T(8,128)}), f32[1,128,128]{2,1,0:T(8,128)}) %reduce-scatter.4.cloned.1.call-update) | async-done | bytes 65552 | tf_op jit(solution)/shard_map/reduce_scatter | solution.py:132
  687.3 218.9 %reduce-scatter.6.cloned.1.call-done = f32[1,128,128]{2,1,0:T(8,128)} async-done(((f32[32,128,128]{2,1,0:T(8,128)}), f32[1,128,128]{2,1,0:T(8,128)}) %reduce-scatter.6.cloned.1.call-update) | async-done | bytes 65552 | tf_op jit(solution)/shard_map/reduce_scatter | solution.py:133
  (123 shorter events, 66.9 us)
Async XLA Ops:
  7.2 95.5 %all-gather.6.cloned.1.call-start = ((), (), s32[]{:S(2)}) async-start(), calls=%async_computation.9 | async-start | bytes 1081344 | tf_op jit(solution)/shard_map/all_gather | solution.py:82
  11.0 9.7 %copy-start.12 = (s32[256,1]{0,1:T(1,128)}, s32[256,1]{0,1:T(1,128)S(1)}, u32[]{:S(2)}) copy-start(s32[256,1]{0,1:T(1,128)S(1)} %compare_select_fusion.1) | copy-start | bytes 3076
  15.5 8.6 copy-start.9
  16.2 18.5 %all-to-all-start = ((bf16[1,8,40]{2,0,1:T(2,128)(2,1)}), bf16[1,8,40]{2,0,1:T(2,128)(2,1)}, u32[]{:S(2)}, u32[]{:S(2)}) async-start(bf16[1,8,40]{2,0,1:T(2,128)(2,1)} %select_n.130), calls=%async_computation | async-start | bytes 8192 | tf_op jit(solution)/shard_map/all_to_all | solution.py:75
  20.7 144.2 %all-gather.8.cloned.1.call-start = ((), (), s32[]{:S(2)}) async-start(), calls=%async_computation.10 | async-start | bytes 1081344 | tf_op jit(solution)/shard_map/all_gather | solution.py:81
  26.8 3.0 copy-start.14
  34.6 30.6 %all-to-all-start.1 = ((bf16[24,8,40,128]{3,2,0,1:T(8,128)(2,1)}), bf16[24,8,40,128]{3,2,0,1:T(8,128)(2,1)S(1)}, u32[]{:S(2)}, u32[]{:S(2)}) async-start(bf16[24,8,40,128]{3,2,0,1:T(8,128)(2,1)} %copy.66), calls=%async_computation.1 | async-start | bytes 3932160 | tf_op jit(solution)/shard_map/all_to_all | solution.py:74
  39.5 201.8 %all-gather.4.cloned.1.call-start = ((), (), s32[]{:S(2)}) async-start(), calls=%async_computation.8 | async-start | bytes 1081344 | tf_op jit(solution)/shard_map/all_gather | solution.py:83
  43.3 26.5 %copy-start.17 = (s32[1,32]{1,0:T(1,128)S(1)}, s32[1,32]{1,0:T(1,128)}, u32[]{:S(2)}) copy-start(s32[1,32]{1,0:T(1,128)} %param.22) | copy-start | bytes 388
  43.3 26.6 %copy-start.18 = (s32[1,32]{1,0:T(1,128)S(1)}, s32[1,32]{1,0:T(1,128)}, u32[]{:S(2)}) copy-start(s32[1,32]{1,0:T(1,128)} %param.24) | copy-start | bytes 388
  43.3 26.6 %copy-start.15 = (s32[1,32]{1,0:T(1,128)S(1)}, s32[1,32]{1,0:T(1,128)}, u32[]{:S(2)}) copy-start(s32[1,32]{1,0:T(1,128)} %param.23) | copy-start | bytes 388
  43.3 26.6 %copy-start.16 = (s32[1,32]{1,0:T(1,128)S(1)}, s32[1,32]{1,0:T(1,128)}, u32[]{:S(2)}) copy-start(s32[1,32]{1,0:T(1,128)} %param.25) | copy-start | bytes 388
  65.2 5.4 copy-start
  65.3 30.1 %all-to-all-start.2 = ((bf16[24,8,40,128]{3,2,0,1:T(8,128)(2,1)}), bf16[24,8,40,128]{3,2,0,1:T(8,128)(2,1)}, u32[]{:S(2)}, u32[]{:S(2)}) async-start(bf16[24,8,40,128]{3,2,0,1:T(8,128)(2,1)} %copy.70), calls=%async_computation.2 | async-start | bytes 3932160 | tf_op jit(solution)/shard_map/all_to_all | solution.py:73
  69.6 398.4 %reduce-scatter.8.cloned.1.call-start = ((), (), s32[]{:S(2)}) async-start(), calls=%async_computation.13 | async-start | bytes 2162688 | tf_op jit(solution)/shard_map/reduce_scatter | solution.py:134
  241.2 10.2 %copy-start.3 = (bf16[32,320,128]{2,1,0:T(8,128)(2,1)S(1)}, bf16[32,320,128]{2,1,0:T(8,128)(2,1)}, u32[]{:S(2)}) copy-start(bf16[32,320,128]{2,1,0:T(8,128)(2,1)} %gather_fusion.7) | copy-start | bytes 7864324
  254.0 433.3 %reduce-scatter.4.cloned.1.call-start = ((), (), s32[]{:S(2)}) async-start(), calls=%async_computation.11 | async-start | bytes 2162688 | tf_op jit(solution)/shard_map/reduce_scatter | solution.py:132
  259.1 647.1 %reduce-scatter.6.cloned.1.call-start = ((), (), s32[]{:S(2)}) async-start(), calls=%async_computation.12 | async-start | bytes 2162688 | tf_op jit(solution)/shard_map/reduce_scatter | solution.py:133
  284.1 7.8 copy-start.1
  287.5 28.4 %all-to-all-start.4 = ((bf16[1,8,40]{2,0,1:T(2,128)(2,1)}), bf16[1,8,40]{2,0,1:T(2,128)(2,1)S(1)}, u32[]{:S(2)}, u32[]{:S(2)}) async-start(bf16[1,8,40]{2,0,1:T(2,128)(2,1)} %convert_element_type.119), calls=%async_computation.4 | async-start | bytes 8192 | tf_op jit(solution)/shard_map/all_to_all | solution.py:123
  315.9 5.0 copy-start.11
  315.9 5.1 copy-start.13
  315.9 7.4 copy-start.7
  315.9 30.8 %all-to-all-start.3 = ((bf16[24,8,40,128]{3,2,0,1:T(8,128)(2,1)}), bf16[24,8,40,128]{3,2,0,1:T(8,128)(2,1)S(1)}, u32[]{:S(2)}, u32[]{:S(2)}) async-start(bf16[24,8,40,128]{3,2,0,1:T(8,128)(2,1)} %copy.74), calls=%async_computation.3 | async-start | bytes 3932160 | tf_op jit(solution)/shard_map/all_to_all | solution.py:116
  (6 other events, 11.8 us)
Sparse Core Ops, SparseCore 0:
  10.6 77.8 all-gather.5
  91.1 73.6 all-gather.7
  167.4 73.7 all-gather.3
  254.1 213.8 reduce-scatter.7
  472.8 214.4 reduce-scatter.3
  691.6 214.5 reduce-scatter.5
where the time goes:
time: 915 us; the launch traced here: 913 us
  waiting for transfers between devices  743 us (81%)
  local copies, waits for them, and re-layouts  52.9 us (6%)
  matrix products  42.8 us (5%)
  other arithmetic  36.5 us (4%)
  starting transfers between devices  23.7 us (3%)
  between operations  14.6 us (2%)
    reduce_scatter x1, waiting for transfers between devices, local(): lax.psum_scatter(gate_part, 'fsdp', scatter_dimension=0, tiled=True)  219 us
    reduce_scatter x1, waiting for transfers between devices, local(): lax.psum_scatter(up_part, 'fsdp', scatter_dimension=0, tiled=True)  219 us
    reduce_scatter x1, waiting for transfers between devices, local(): lax.psum_scatter(down_part, 'fsdp', scatter_dimension=0, tiled=True)  115 us
    all_gather x1, waiting for transfers between devices, local(): lax.all_gather(down_tiles, 'fsdp', axis=1, tiled=True)  71.1 us
    all_gather x1, waiting for transfers between devices, local(): lax.all_gather(gate_tiles, 'fsdp', axis=1, tiled=True)  56.9 us
    all_to_all x1, waiting for transfers between devices, local(): lax.all_to_all(part.reshape(row_blocks, groups, capacity, tile), 'expert'...  22.8 us
    scatter-add x2, other arithmetic, place_terms(): jnp.zeros((blocks,) + terms.shape[1:], jnp.float32).at[index_to].add(terms)  22.6 us
    all_to_all x1, waiting for transfers between devices, local(): lax.all_to_all(spread(cotangent), 'expert', split_axis=1, concat_axis=1,...  21.9 us
  transfers between devices with their start and end apart: 11, of which 8 were waited for; matrix products, arithmetic and copies ran while one was open for 13% of the time, Pallas kernels for 0%

commit v1 on v0

v1 whole, which is shorter than its diff:
```python
import functools

import jax
import jax.numpy as jnp
from jax import lax
from jax.experimental import pallas as pl
from jax.experimental.pallas import tpu as pltpu
from jax.sharding import Mesh
from jax.sharding import PartitionSpec as P

FF = 8192
TILE = 128
COL_BLOCKS = FF // TILE
EXPERTS = 8
NX = 4
NZ = 8
SLOTS = NX * NZ
CAP = 40
ROWS = 128
WIDTH = 3072
TOTAL = EXPERTS * CAP
PEERS = EXPERTS * NX
AHEAD = 16
IN_AT, OUT_AT, Z_AT, COUNT_AT, RANK_AT, PLAN = 0, 32, 64, 96, 128, 256

BF = jnp.bfloat16
F32 = jnp.float32
SMEM = pl.BlockSpec(memory_space=pltpu.SMEM)
VMEM = pl.BlockSpec(memory_space=pltpu.VMEM)
LIMIT = 48 * 1024 * 1024


def call(kernel, out, ins, outs, scratch=(), cost=None):
    return pl.pallas_call(
        kernel,
        out_shape=out,
        in_specs=ins,
        out_specs=outs,
        scratch_shapes=list(scratch),
        cost_estimate=cost,
        compiler_params=pltpu.CompilerParams(vmem_limit_bytes=LIMIT),
    )


def dot(a, b):
    return lax.dot_general(a, b, (((1,), (0,)), ((), ())), preferred_element_type=F32)


def dot_nt(a, b):
    return lax.dot_general(a, b, (((1,), (1,)), ((), ())), preferred_element_type=F32)


def dot_tn(a, b):
    return lax.dot_general(a, b, (((0,), (0,)), ((), ())), preferred_element_type=F32)


def back_tail(per):
    return 16 if per % 2 == 0 else 8


def plan_kernel(in_ids, in_count, out_ids, out_count, plan):
    def clear(i, _):
        plan[0, i] = 0
        return 0

    lax.fori_loop(0, PLAN, clear, 0)

    def step(i, rank):
        s = (i % NX) * NZ + i // NX
        live = jnp.logical_and(in_count[0, s] > 0, out_count[0, s] > 0)
        plan[0, RANK_AT + s] = jnp.where(live, rank, -1)

        @pl.when(live)
        def _():
            plan[0, IN_AT + rank] = in_ids[0, s] // COL_BLOCKS
            plan[0, OUT_AT + rank] = out_ids[0, s]
            plan[0, Z_AT + rank] = i // NX

        return rank + live.astype(jnp.int32)

    plan[0, COUNT_AT] = lax.fori_loop(0, SLOTS, step, jnp.int32(0))


def assignment(ids):
    experts = lax.broadcasted_iota(jnp.int32, (EXPERTS, ROWS), 0)
    first = ids[0:1, :] == experts
    second = ids[1:2, :] == experts
    named = jnp.logical_or(first, second)
    above = lax.broadcasted_iota(jnp.int32, (ROWS, ROWS), 0) < lax.broadcasted_iota(
        jnp.int32, (ROWS, ROWS), 1
    )
    place = dot(named.astype(F32).astype(BF), above.astype(F32).astype(BF))
    return first, second, jnp.where(named, place, -1.0)


def one_hot(place):
    at = lax.broadcasted_iota(jnp.int32, (CAP, ROWS), 0).astype(F32)
    rows = [(place[e : e + 1, :] == at).astype(F32) for e in range(EXPERTS)]
    return jnp.concatenate(rows, axis=0).astype(BF)


def dispatch_kernel(per, plans, ids, probs, tokens, cot, out, xs, ys, prob_rows, places):
    first, second, place = assignment(ids[...])
    p = probs[...].astype(F32)
    prob_rows[...] = jnp.where(first, p[0:1, :], 0.0) + jnp.where(second, p[1:2, :], 0.0)
    places[...] = place
    pick = one_hot(place)
    for j in range(WIDTH // 256):
        at = slice(j * 256, (j + 1) * 256)
        xs[:, at] = dot(pick, tokens[:, at])
        ys[:, at] = dot(pick, cot[:, at])
    line = lax.broadcasted_iota(jnp.int32, (AHEAD, ROWS), 0)

    def per_expert(e, _):
        rows = pl.ds(pl.multiple_of(e * CAP, 8), CAP)
        extra = jnp.where(
            line == 0,
            prob_rows[pl.ds(e, 1), :],
            jnp.where(line == 1, places[pl.ds(e, 1), :], 0.0),
        ).astype(BF)
        for x in range(NX):
            for k in range(per):
                r = k * NX + x
                at_in = pl.multiple_of(plans[e, IN_AT + r] * TILE, TILE)
                at_out = pl.multiple_of(plans[e, OUT_AT + r] * TILE, TILE)
                both = jnp.concatenate(
                    [xs[rows, pl.ds(at_in, TILE)], ys[rows, pl.ds(at_out, TILE)]], axis=0
                )
                out[e * NX + x, 2 * CAP * k : 2 * CAP * (k + 1), :] = both.astype(BF)
            out[e * NX + x, 2 * CAP * per : 2 * CAP * per + AHEAD, :] = extra
        return 0

    lax.fori_loop(0, EXPERTS, per_expert, 0)


def pick_weights_kernel(plan, place, own, one, two, three, out):
    x, z = place[0], place[1]
    out[...] = jnp.zeros_like(out)
    for shift, source in enumerate((own, one, two, three)):
        home = lax.rem(x + NX - shift, NX)
        rank = plan[0, RANK_AT + home * NZ + z]

        @pl.when(jnp.logical_and(rank >= 0, lax.rem(rank + NX, NX) == x))
        def _():
            out[...] = source[...]


def pick_grads_kernel(plan, place, own, one, two, three, gate, up, down):
    x, z = place[0], place[1]
    rank = plan[0, RANK_AT + x * NZ + z]
    outs = (gate, up, down)
    for ref in outs:
        ref[...] = jnp.zeros_like(ref)
    for shift, source in enumerate((own, one, two, three)):
        home = lax.rem(x + NX - shift, NX)

        @pl.when(jnp.logical_and(rank >= 0, lax.rem(rank + NX, NX) == home))
        def _():
            for i, ref in enumerate(outs):
                ref[0, 0] = source[i]


def expert_kernel(per, plan, place, got, weights, back, grads, pair, down, pair_sum, down_sum):
    x = place[0]
    count = plan[0, COUNT_AT]
    for k in range(per):
        z = plan[0, Z_AT + k * NX + x]
        live = jnp.where(k * NX + x < count, 1.0, 0.0).astype(F32)
        for i in range(2):
            tile = weights[3 * z + i].astype(F32) * live
            pair[k, :, i * TILE : (i + 1) * TILE] = tile.astype(BF)
        down[k] = (weights[3 * z + 2].astype(F32) * live).astype(BF)
    pair_sum[...] = jnp.zeros_like(pair_sum)
    down_sum[...] = jnp.zeros_like(down_sum)
    group = 8
    rows = group * CAP
    tail = back_tail(per)
    ones = jnp.ones((ROWS, TILE), BF)

    def chunk(c, _):
        at = pl.ds(c * group, group)
        extra = got[at, 2 * CAP * per : 2 * CAP * per + AHEAD, :].astype(F32)
        slot = lax.broadcasted_iota(jnp.int32, (group, CAP, ROWS), 1).astype(F32)
        mine = extra[:, 1:2, :] == slot
        p = dot(jnp.where(mine, extra[:, 0:1, :], 0.0).reshape(rows, ROWS).astype(BF), ones)
        inner = jnp.zeros((rows, TILE), F32)
        pieces = []
        for k in range(per):
            both = got[at, 2 * CAP * k : 2 * CAP * (k + 1), :].astype(F32)
            rows_x = both[:, :CAP, :].reshape(rows, TILE).astype(BF)
            rows_dy = both[:, CAP:, :].reshape(rows, TILE)
            gu = dot(rows_x, pair[k])
            g, u = gu[:, :TILE], gu[:, TILE:]
            m = dot_nt(rows_dy.astype(BF), down[k])
            sig = jax.nn.sigmoid(g)
            act = g * sig
            h = (act * u).astype(BF)
            inner = inner + h.astype(F32) * m
            dh = p * m
            dg = (dh * u * sig * (1.0 + g * (1.0 - sig))).astype(BF)
            du = (dh * act).astype(BF)
            q = (p * rows_dy).astype(BF)
            dgu = jnp.concatenate([dg, du], axis=1)
            pieces.append(dot_nt(dgu, pair[k]).reshape(group, CAP, TILE))
            pair_sum[k] += dot_tn(rows_x, dgu)
            down_sum[k] += dot_tn(h, q)
        column = jnp.sum(inner, axis=1, keepdims=True).reshape(group, CAP, 1)
        row = jnp.sum(jnp.where(mine, column, 0.0), axis=1, keepdims=True)
        high = row.astype(BF).astype(F32)
        line = lax.broadcasted_iota(jnp.int32, (group, tail, ROWS), 1)
        pieces.append(jnp.where(line == 0, high, jnp.where(line == 1, row - high, 0.0)))
        back[at] = jnp.concatenate(pieces, axis=1).astype(BF)
        return 0

    lax.fori_loop(0, PEERS // group, chunk, 0)
    grads[...] = jnp.zeros_like(grads)
    for k in range(per):
        z = plan[0, Z_AT + k * NX + x]

        @pl.when(k * NX + x < count)
        def _():
            grads[3 * z] = pair_sum[k, :, :TILE]
            grads[3 * z + 1] = pair_sum[k, :, TILE:]
            grads[3 * z + 2] = down_sum[k]


def combine_kernel(per, plans, ids, back, token_grad, prob_grad, parts, prob_rows):
    tail = back_tail(per)
    parts[...] = jnp.zeros_like(parts)

    def per_expert(e, _):
        rows = pl.ds(pl.multiple_of(e * CAP, 8), CAP)
        total = jnp.zeros((1, ROWS), F32)
        for x in range(NX):
            chunk = back[e * NX + x].astype(F32)
            for k in range(per):
                at = pl.multiple_of(plans[e, IN_AT + k * NX + x] * TILE, TILE)
                parts[rows, pl.ds(at, TILE)] += chunk[CAP * k : CAP * (k + 1), :]
            total = total + chunk[CAP * per : CAP * per + 1] + chunk[CAP * per + 1 : CAP * per + 2]
        prob_rows[pl.ds(e, 1), :] = total
        return 0

    lax.fori_loop(0, EXPERTS, per_expert, 0)
    first, second, place = assignment(ids[...])
    pick = one_hot(place)
    for j in range(WIDTH // 256):
        at = slice(j * 256, (j + 1) * 256)
        token_grad[:, at] = dot_tn(pick, parts[:, at].astype(BF)).astype(BF)
    rows = prob_rows[...]
    prob_grad[0:1, :] = jnp.sum(jnp.where(first, rows, 0.0), axis=0, keepdims=True)
    prob_grad[1:2, :] = jnp.sum(jnp.where(second, rows, 0.0), axis=0, keepdims=True)


def exchange(values, axes):
    return lax.all_to_all(values, axes, split_axis=0, concat_axis=0, tiled=True)


def shifted(values):
    return [
        lax.ppermute(values, "x", [(i, (i + shift) % NX) for i in range(NX)])
        for shift in range(1, NX)
    ]


def rest(per, plan, plans, place, ids, probs, tokens, cotangent, weights):
    shape = jax.ShapeDtypeStruct
    ahead = 2 * CAP * per + AHEAD
    behind = CAP * per + back_tail(per)
    sent = call(
        functools.partial(dispatch_kernel, per),
        shape((PEERS, ahead, TILE), BF),
        [SMEM, VMEM, VMEM, VMEM, VMEM],
        VMEM,
        [
            pltpu.VMEM((TOTAL, WIDTH), F32),
            pltpu.VMEM((TOTAL, WIDTH), F32),
            pltpu.VMEM((EXPERTS, ROWS), F32),
            pltpu.VMEM((EXPERTS, ROWS), F32),
        ],
    )(plans, ids, probs, tokens, cotangent)
    got = exchange(sent, ("expert", "x"))
    weights = lax.all_gather(weights, "z", axis=0, tiled=True)
    back, grads = call(
        functools.partial(expert_kernel, per),
        (shape((PEERS, behind, TILE), BF), shape((3 * NZ, TILE, TILE), F32)),
        [SMEM, SMEM, VMEM, VMEM],
        (VMEM, VMEM),
        [
            pltpu.VMEM((per, TILE, 2 * TILE), BF),
            pltpu.VMEM((per, TILE, TILE), BF),
            pltpu.VMEM((per, TILE, 2 * TILE), F32),
            pltpu.VMEM((per, TILE, TILE), F32),
        ],
    )(plan, place, got, weights)
    grads = lax.psum_scatter(grads, "z", scatter_dimension=0, tiled=True)
    returned = exchange(back, ("expert", "x"))
    token_grad, prob_grad = call(
        functools.partial(combine_kernel, per),
        (shape((ROWS, WIDTH), BF), shape((2, ROWS), F32)),
        [SMEM, VMEM, VMEM],
        (VMEM, VMEM),
        [pltpu.VMEM((TOTAL, WIDTH), F32), pltpu.VMEM((EXPERTS, ROWS), F32)],
    )(plans, ids, returned)
    tile = shape((1, 1, TILE, TILE), F32)
    gate, up, down = call(
        pick_grads_kernel,
        (tile, tile, tile),
        [SMEM, SMEM, VMEM, VMEM, VMEM, VMEM],
        (VMEM, VMEM, VMEM),
    )(plan, place, grads, *shifted(grads))
    return token_grad, prob_grad, gate, up, down


def local(
    tokens,
    cotangent,
    expert_ids,
    probs,
    gate_tiles,
    up_tiles,
    down_tiles,
    in_ids,
    in_count,
    out_ids,
    out_count,
):
    shape = jax.ShapeDtypeStruct
    plan = call(plan_kernel, shape((1, PLAN), jnp.int32), [SMEM] * 4, SMEM)(
        in_ids, in_count, out_ids, out_count
    )
    plans = exchange(jnp.broadcast_to(plan, (EXPERTS, PLAN)), "expert")
    place = jnp.stack([lax.axis_index("x"), lax.axis_index("z")]).astype(jnp.int32)
    ids = expert_ids.T
    rows = probs.T
    own = jnp.concatenate([gate_tiles[0], up_tiles[0], down_tiles[0]], axis=0)
    weights = call(
        pick_weights_kernel,
        shape((3, TILE, TILE), BF),
        [SMEM, SMEM, VMEM, VMEM, VMEM, VMEM],
        VMEM,
    )(plan, place, own, *shifted(own))
    most = jnp.max(plans[:, COUNT_AT])
    sizes = (3, 4, 8)
    which = sum((most > NX * size).astype(jnp.int32) for size in sizes[:-1])
    token_grad, prob_grad, gate, up, down = lax.switch(
        which,
        [functools.partial(rest, size) for size in sizes],
        plan,
        plans,
        place,
        ids,
        rows,
        tokens,
        cotangent,
        weights,
    )
    return token_grad, prob_grad.T.astype(BF), gate, up, down


def solution(mesh):
    finer = Mesh(mesh.devices.reshape(EXPERTS, NX, NZ), ("expert", "x", "z"))
    rows = P(("expert", "x", "z"), None)
    tiles = P("expert", ("x", "z"), None, None)
    table = P("expert", None)
    return jax.shard_map(
        local,
        mesh=finer,
        in_specs=(rows, rows, rows, rows, tiles, tiles, tiles, table, table, table, table),
        out_specs=(rows, rows, tiles, tiles, tiles),
        check_vma=False,
    )
```

time: 915 us -> 150 us (0.16)
  waiting for transfers between devices: 743 us -> 46.7 us
  local copies, waits for them, and re-layouts: 52.9 us -> 5.69 us
  matrix products: 42.8 us -> 0 us
  other arithmetic: 36.5 us -> 2.76 us
  blocking collectives: 0 us -> 29.2 us
  Pallas kernels: 0 us -> 23 us
    reduce_scatter x3 -> x1, waiting for transfers between devices: 554 us -> 35.1 us  [rest(): grads = lax.psum_scatter(grads, 'z', scatter_dimension=0, tiled=True)]
    all_gather x3 -> x0, waiting for transfers between devices: 128 us -> none  [the longest x1 71.1 us: local(): lax.all_gather(down_tiles, 'fsdp', axis=1, tiled=True)]
    all_to_all x5 -> x3, waiting for transfers between devices: 59 us -> 10.4 us  [exchange(): return lax.all_to_all(values, axes, split_axis=0, concat_axis=0, tiled=True)]
    dot_general x9 -> x0, matrix products: 42.8 us -> none  [the longest x3 15.5 us: forward_product(): jnp.einsum('sri,sij->srj', picked, tiles, preferred_element_type=jnp.floa...]
    all_gather x0 -> x1, blocking collectives: none -> 29.2 us  [rest(): weights = lax.all_gather(weights, 'z', axis=0, tiled=True)]
    pallas_call x0 -> x6, Pallas kernels: none -> 23 us  [the longest x1 9.16 us: rest(): call(functools.partial(expert_kernel, per), (shape((PEERS, behind, TILE),...]
    gather x9 -> x0, local copies, waits for them, and re-layouts: 22.6 us -> none  [the longest x2 5.3 us: spread(): jnp.take(blocked, token_of, axis=1)]
    scatter-add x2 -> x0, other arithmetic: 22.6 us -> none  [place_terms(): jnp.zeros((blocks,) + terms.shape[1:], jnp.float32).at[index_to].add(terms)]
  transfers between devices with their start and end apart: 11 -> 10, of which waited for: 8 -> 4; matrix products, arithmetic and copies ran while one was open for 13% -> 1% of each run, Pallas kernels for 0% -> 5%
where the time goes in v1:
time: 150 us; the launch traced here: 148 us
  waiting for transfers between devices  46.7 us (31%)
  blocking collectives  29.2 us (19%)
  starting transfers between devices  24.7 us (16%)
  Pallas kernels  23 us (15%)
  between operations  15.4 us (10%)
  local copies, waits for them, and re-layouts  5.69 us (4%)
  other arithmetic  2.76 us (2%)
    reduce_scatter x1, waiting for transfers between devices, rest(): grads = lax.psum_scatter(grads, 'z', scatter_dimension=0, tiled=True)  35.1 us
    all_gather x1, blocking collectives, rest(): weights = lax.all_gather(weights, 'z', axis=0, tiled=True)  29.2 us
    all_to_all x3, starting transfers between devices, exchange(): return lax.all_to_all(values, axes, split_axis=0, concat_axis=0, tiled=True)  14 us
    ppermute x6, starting transfers between devices, shifted(): lax.ppermute(values, 'x', [(i, (i + shift) % NX) for i in range(NX)])  10.7 us
    all_to_all x3, waiting for transfers between devices, exchange(): return lax.all_to_all(values, axes, split_axis=0, concat_axis=0, tiled=True)  10.4 us
    pallas_call x1, Pallas kernels, rest(): call(functools.partial(expert_kernel, per), (shape((PEERS, behind, TILE),...  9.16 us
    pallas_call x1, Pallas kernels, rest(): call(functools.partial(dispatch_kernel, per), shape((PEERS, ahead, TILE),...  5 us
    pallas_call x1, Pallas kernels, local(): call(plan_kernel, shape((1, PLAN), jnp.int32), [SMEM] * 4, SMEM)  3.6 us
  transfers between devices with their start and end apart: 10, of which 4 were waited for; matrix products, arithmetic and copies ran while one was open for 1% of the time, Pallas kernels for 5%

profile of v1, /device:TPU:32, one launch (start us, length us, event | category | flops | bytes accessed | tf_op | source)
XLA Modules:
  0.0 147.6 jit_solution(13603804420166707363)
XLA Ops:
  7.2 0.8 pad_maximum_fusion.own
  8.0 3.1 %collective-permute-start.10 = (bf16[3,128,128]{2,1,0:T(8,128)(2,1)S(1)}, bf16[3,128,128]{2,1,0:T(8,128)(2,1)S(1)}, u32[]{:S(2)}, u32[]{:S(2)}) collective-permute-start(bf16[3,128,128]{2,1,0:T(8,128)(2,1)S(1)} %pad_maximum_fusion.own), channel_id=1, source_target_pairs={{0,16},{8,24},{16,0},{24,8},{1,17},{9,25},{17,1},{25,9},{2,18},{10... | collective-permute-start | bytes 294920 | tf_op jit(solution)/shard_map/ppermute | solution.py:260
  11.1 1.1 collective-permute-start.11
  12.2 0.9 collective-permute-start.9
  15.7 3.6 %shard_map.146.plan = s32[1,256]{1,0:T(1,128)S(1)} custom-call(s32[1,32]{1,0:T(1,128)S(1)} %copy-done.8, s32[1,32]{1,0:T(1,128)S(1)} %copy-done.9, s32[1,32]{1,0:T(1,128)S(1)} %copy-done.10, s32[1,32]{1,0:T(1,128)S(1)} %copy-done.11), custom_call_target="tpu_custom_call" | custom-call | tf_op jit(solution)/shard_map/pallas_call | solution.py:328
  19.9 4.5 %all-to-all-start.6 = ((s32[8,1,256]{2,1,0:T(1,128)}), s32[8,1,256]{2,1,0:T(1,128)S(1)}, u32[]{:S(2)}, u32[]{:S(2)}) async-start(s32[8,1,256]{2,1,0:T(1,128)} %broadcast_in_dim.2), calls=%async_computation.9 | async-start | bytes 16384 | tf_op jit(solution)/shard_map/all_to_all | solution.py:255
  24.5 5.2 %all-to-all-done.6 = s32[8,1,256]{2,1,0:T(1,128)S(1)} async-done(((s32[8,1,256]{2,1,0:T(1,128)}), s32[8,1,256]{2,1,0:T(1,128)S(1)}, u32[]{:S(2)}, u32[]{:S(2)}) %all-to-all-start.6) | async-done | bytes 8224 | tf_op jit(solution)/shard_map/all_to_all | solution.py:255
  32.4 107.2 %conditional.1 = (bf16[128,3072]{1,0:T(8,128)(2,1)}, f32[2,128]{1,0:T(2,128)}, f32[1,1,128,128]{3,2,1,0:T(8,128)}, f32[1,1,128,128]{3,2,1,0:T(8,128)}, f32[1,1,128,128]{3,2,1,0:T(8,128)}) conditional(s32[]{:T(128)} %clamp.3, (s32[8,256]{1,0:T(8,128)S(1)}, s32[2,128]{1,0:T(2,128)}, bf16[2,128]{1,0:T(2,128)(2,1)}, ...), branch_computations={%region_1.0_spmd, %region_3.0_spmd, %region_5.0_spmd} | conditional | bytes 66228660 | solution.py:345
  32.4 5.0 %branch_1_fun.4 = bf16[32,336,128]{2,1,0:T(8,128)(2,1)} custom-call(s32[8,256]{1,0:T(8,128)S(1)} %get-tuple-element.63.plans, s32[2,128]{1,0:T(2,128)} %get-tuple-element.64.ids, bf16[2,128]{1,0:T(2,128)(2,1)} %get-tuple-element.67.probs, bf16[128,3072]{1,0:T(8,128)(2,1)} %get-tuple-element.68.tokens, bf16[128,3072]{1,0:T(8,128)(2,1)} %get-tuple-element.69.cot), custom_call_target="tpu_custom_call" | custom-call | tf_op jit(solution)/shard_map/cond/branch_1_fun/pallas_call | solution.py:269
  37.5 4.6 %all-to-all-start.2 = ((bf16[32,336,128]{2,1,0:T(8,128)(2,1)}), bf16[32,336,128]{2,1,0:T(8,128)(2,1)S(1)}, u32[]{:S(2)}, u32[]{:S(2)}) async-start(bf16[32,336,128]{2,1,0:T(8,128)(2,1)} %branch_1_fun.4), calls=%async_computation.3 | async-start | bytes 5505024 | tf_op jit(solution)/shard_map/cond/branch_1_fun/all_to_all | solution.py:255
  42.1 29.2 %all_gather.7.weights = bf16[24,128,128]{2,1,0:T(8,128)(2,1)S(1)} all-gather(bf16[3,128,128]{2,1,0:T(8,128)(2,1)} %copy-done.13), channel_id=1, replica_groups=mesh['expert'=8,'x'=4,'z'=8] {'z'}, dimensions={0}, use_global_device_ids=true | all-gather | bytes 884736 | tf_op jit(solution)/shard_map/cond/branch_1_fun/all_gather | solution.py:282
  71.4 5.2 %all-to-all-done.2.got = bf16[32,336,128]{2,1,0:T(8,128)(2,1)S(1)} async-done(((bf16[32,336,128]{2,1,0:T(8,128)(2,1)}), bf16[32,336,128]{2,1,0:T(8,128)(2,1)S(1)}, u32[]{:S(2)}, u32[]{:S(2)}) %all-to-all-start.2) | async-done | bytes 2752544 | tf_op jit(solution)/shard_map/cond/branch_1_fun/all_to_all | solution.py:255
  76.6 1.5 %copy-done.12 = bf16[32,336,128]{2,1,0:T(8,128)(2,1)} copy-done((bf16[32,336,128]{2,1,0:T(8,128)(2,1)}, bf16[32,336,128]{2,1,0:T(8,128)(2,1)S(1)}, u32[]{:S(2)}) %copy-start.12) | copy-done | bytes 2752536 | tf_op jit(solution)/shard_map/cond
  78.1 9.2 %branch_1_fun.5 = (bf16[32,176,128]{2,1,0:T(8,128)(2,1)}, f32[24,128,128]{2,1,0:T(8,128)}) custom-call(s32[1,256]{1,0:T(1,128)S(1)} %get-tuple-element.65.plan, s32[2]{0:T(128)} %copy-done.17, bf16[32,336,128]{2,1,0:T(8,128)(2,1)} %copy-done.12, bf16[24,128,128]{2,1,0:T(8,128)(2,1)S(1)} %all_gather.7.weights), custom_call_target="tpu_custom_call" | custom-call | tf_op jit(solution)/shard_map/cond/branch_1_fun/pallas_call | solution.py:283
  87.3 4.9 %all-to-all-start.3 = ((bf16[32,176,128]{2,1,0:T(8,128)(2,1)}), bf16[32,176,128]{2,1,0:T(8,128)(2,1)S(1)}, u32[]{:S(2)}, u32[]{:S(2)}) async-start(bf16[32,176,128]{2,1,0:T(8,128)(2,1)} %get-tuple-element.71), calls=%async_computation.4 | async-start | bytes 2883584 | tf_op jit(solution)/shard_map/cond/branch_1_fun/all_to_all | solution.py:255
  92.2 35.1 %reduce-scatter.6.cloned.1.call-done.own = f32[3,128,128]{2,1,0:T(8,128)} async-done(((f32[24,128,128]{2,1,0:T(8,128)}), f32[3,128,128]{2,1,0:T(8,128)}) %reduce-scatter.6.cloned.1.call-update) | async-done | bytes 196624 | tf_op jit(solution)/shard_map/cond/branch_1_fun/reduce_scatter | solution.py:295
  127.3 1.4 collective-permute-start.3
  128.7 2.6 %collective-permute-start.4 = (f32[3,128,128]{2,1,0:T(8,128)}, f32[3,128,128]{2,1,0:T(8,128)S(1)}, u32[]{:S(2)}, u32[]{:S(2)}) collective-permute-start(f32[3,128,128]{2,1,0:T(8,128)} %reduce-scatter.6.cloned.1.call-done.own), channel_id=1, source_target_pairs={{0,16},{8,24},{16,0},{24,8},{1,17},{9,25},{17,1},{25,9},{2,18},{10... | collective-permute-start | bytes 589832 | tf_op jit(solution)/shard_map/cond/branch_1_fun/ppermute | solution.py:260
  131.4 1.5 %collective-permute-start.5 = (f32[3,128,128]{2,1,0:T(8,128)}, f32[3,128,128]{2,1,0:T(8,128)S(1)}, u32[]{:S(2)}, u32[]{:S(2)}) collective-permute-start(f32[3,128,128]{2,1,0:T(8,128)} %reduce-scatter.6.cloned.1.call-done.own), channel_id=1, source_target_pairs={{0,24},{8,0},{16,8},{24,16},{1,25},{9,1},{17,9},{25,17},{2,26},{10... | collective-permute-start | bytes 589832 | tf_op jit(solution)/shard_map/cond/branch_1_fun/ppermute | solution.py:260
  132.9 3.4 %branch_1_fun.6 = (bf16[128,3072]{1,0:T(8,128)(2,1)}, f32[2,128]{1,0:T(2,128)}) custom-call(s32[8,256]{1,0:T(8,128)S(1)} %get-tuple-element.63.plans, s32[2,128]{1,0:T(2,128)S(1)} %copy-done.15, bf16[32,176,128]{2,1,0:T(8,128)(2,1)S(1)} %all-to-all-done.3.back), custom_call_target="tpu_custom_call" | custom-call | tf_op jit(solution)/shard_map/cond/branch_1_fun/pallas_call | solution.py:297
  136.3 1.1 collective-permute-done.4.two
  137.4 0.9 copy-done.6
  138.3 1.3 branch_1_fun.7
  139.6 1.2 convert_bitcast_fusion
  (31 shorter events, 4.7 us)
Async XLA Ops:
  8.0 23.8 %collective-permute-start.10 = (bf16[3,128,128]{2,1,0:T(8,128)(2,1)S(1)}, bf16[3,128,128]{2,1,0:T(8,128)(2,1)S(1)}, u32[]{:S(2)}, u32[]{:S(2)}) collective-permute-start(bf16[3,128,128]{2,1,0:T(8,128)(2,1)S(1)} %pad_maximum_fusion.own), channel_id=1, source_target_pairs={{0,16},{8,24},{16,0},{24,8},{1,17},{9,25},{17,1},{25,9},{2,18},{10... | collective-permute-start | bytes 294920 | tf_op jit(solution)/shard_map/ppermute | solution.py:260
  11.1 20.7 %collective-permute-start.11 = (bf16[3,128,128]{2,1,0:T(8,128)(2,1)S(1)}, bf16[3,128,128]{2,1,0:T(8,128)(2,1)S(1)}, u32[]{:S(2)}, u32[]{:S(2)}) collective-permute-start(bf16[3,128,128]{2,1,0:T(8,128)(2,1)S(1)} %pad_maximum_fusion.own), channel_id=1, source_target_pairs={{0,24},{8,0},{16,8},{24,16},{1,25},{9,1},{17,9},{25,17},{2,26},{10... | collective-permute-start | bytes 294920 | tf_op jit(solution)/shard_map/ppermute | solution.py:260
  12.2 19.5 %collective-permute-start.9 = (bf16[3,128,128]{2,1,0:T(8,128)(2,1)S(1)}, bf16[3,128,128]{2,1,0:T(8,128)(2,1)S(1)}, u32[]{:S(2)}, u32[]{:S(2)}) collective-permute-start(bf16[3,128,128]{2,1,0:T(8,128)(2,1)S(1)} %pad_maximum_fusion.own), channel_id=1, source_target_pairs={{0,8},{8,16},{16,24},{24,0},{1,9},{9,17},{17,25},{25,1},{2,10},{10... | collective-permute-start | bytes 294920 | tf_op jit(solution)/shard_map/ppermute | solution.py:260
  13.1 0.7 copy-start.8
  13.8 0.7 copy-start.9
  14.4 0.7 copy-start.10
  15.1 0.7 copy-start.11
  19.9 9.8 %all-to-all-start.6 = ((s32[8,1,256]{2,1,0:T(1,128)}), s32[8,1,256]{2,1,0:T(1,128)S(1)}, u32[]{:S(2)}, u32[]{:S(2)}) async-start(s32[8,1,256]{2,1,0:T(1,128)} %broadcast_in_dim.2), calls=%async_computation.9 | async-start | bytes 16384 | tf_op jit(solution)/shard_map/all_to_all | solution.py:255
  32.4 5.0 %copy-start.13 = (bf16[3,128,128]{2,1,0:T(8,128)(2,1)}, bf16[3,128,128]{2,1,0:T(8,128)(2,1)S(1)}, u32[]{:S(2)}) copy-start(bf16[3,128,128]{2,1,0:T(8,128)(2,1)S(1)} %get-tuple-element.70) | copy-start | bytes 294916 | tf_op jit(solution)/shard_map/cond
  32.4 5.0 %copy-start.17 = (s32[2]{0:T(128)}, s32[2]{0:T(128)S(1)}, u32[]{:S(2)}) copy-start(s32[2]{0:T(128)S(1)} %get-tuple-element.66.place) | copy-start | bytes 28 | tf_op jit(solution)/shard_map/cond
  37.5 39.1 %all-to-all-start.2 = ((bf16[32,336,128]{2,1,0:T(8,128)(2,1)}), bf16[32,336,128]{2,1,0:T(8,128)(2,1)S(1)}, u32[]{:S(2)}, u32[]{:S(2)}) async-start(bf16[32,336,128]{2,1,0:T(8,128)(2,1)} %branch_1_fun.4), calls=%async_computation.3 | async-start | bytes 5505024 | tf_op jit(solution)/shard_map/cond/branch_1_fun/all_to_all | solution.py:255
  42.1 85.2 %reduce-scatter.6.cloned.1.call-start = ((), (), s32[]{:S(2)}) async-start(), calls=%async_computation.11 | async-start | bytes 1769472 | tf_op jit(solution)/shard_map/cond/branch_1_fun/reduce_scatter | solution.py:295
  76.6 1.5 %copy-start.12 = (bf16[32,336,128]{2,1,0:T(8,128)(2,1)}, bf16[32,336,128]{2,1,0:T(8,128)(2,1)S(1)}, u32[]{:S(2)}) copy-start(bf16[32,336,128]{2,1,0:T(8,128)(2,1)S(1)} %all-to-all-done.2.got) | copy-start | bytes 8257540 | tf_op jit(solution)/shard_map/cond
  87.3 45.6 %copy-start.15 = (s32[2,128]{1,0:T(2,128)S(1)}, s32[2,128]{1,0:T(2,128)}, u32[]{:S(2)}) copy-start(s32[2,128]{1,0:T(2,128)} %get-tuple-element.64.ids) | copy-start | bytes 3076 | tf_op jit(solution)/shard_map/cond
  87.3 50.1 %copy-start.18 = (s32[2]{0:T(128)S(1)}, s32[2]{0:T(128)}, u32[]{:S(2)}) copy-start(s32[2]{0:T(128)} %copy-done.17) | copy-start | bytes 28 | tf_op jit(solution)/shard_map/cond
  87.3 45.6 %all-to-all-start.3 = ((bf16[32,176,128]{2,1,0:T(8,128)(2,1)}), bf16[32,176,128]{2,1,0:T(8,128)(2,1)S(1)}, u32[]{:S(2)}, u32[]{:S(2)}) async-start(bf16[32,176,128]{2,1,0:T(8,128)(2,1)} %get-tuple-element.71), calls=%async_computation.4 | async-start | bytes 2883584 | tf_op jit(solution)/shard_map/cond/branch_1_fun/all_to_all | solution.py:255
  127.3 9.0 %collective-permute-start.3 = (f32[3,128,128]{2,1,0:T(8,128)}, f32[3,128,128]{2,1,0:T(8,128)S(1)}, u32[]{:S(2)}, u32[]{:S(2)}) collective-permute-start(f32[3,128,128]{2,1,0:T(8,128)} %reduce-scatter.6.cloned.1.call-done.own), channel_id=1, source_target_pairs={{0,8},{8,16},{16,24},{24,0},{1,9},{9,17},{17,25},{25,1},{2,10},{10... | collective-permute-start | bytes 589832 | tf_op jit(solution)/shard_map/cond/branch_1_fun/ppermute | solution.py:260
  128.7 8.6 %collective-permute-start.4 = (f32[3,128,128]{2,1,0:T(8,128)}, f32[3,128,128]{2,1,0:T(8,128)S(1)}, u32[]{:S(2)}, u32[]{:S(2)}) collective-permute-start(f32[3,128,128]{2,1,0:T(8,128)} %reduce-scatter.6.cloned.1.call-done.own), channel_id=1, source_target_pairs={{0,16},{8,24},{16,0},{24,8},{1,17},{9,25},{17,1},{25,9},{2,18},{10... | collective-permute-start | bytes 589832 | tf_op jit(solution)/shard_map/cond/branch_1_fun/ppermute | solution.py:260
  131.4 6.0 %collective-permute-start.5 = (f32[3,128,128]{2,1,0:T(8,128)}, f32[3,128,128]{2,1,0:T(8,128)S(1)}, u32[]{:S(2)}, u32[]{:S(2)}) collective-permute-start(f32[3,128,128]{2,1,0:T(8,128)} %reduce-scatter.6.cloned.1.call-done.own), channel_id=1, source_target_pairs={{0,24},{8,0},{16,8},{24,16},{1,25},{9,1},{17,9},{25,17},{2,26},{10... | collective-permute-start | bytes 589832 | tf_op jit(solution)/shard_map/cond/branch_1_fun/ppermute | solution.py:260
  137.4 0.9 copy-start.6
Sparse Core Ops, SparseCore 0:
  87.4 39.8 reduce-scatter.5
